TPU v7x, 32 devices: a whole 2x2x4 slice. The times are simulated.
32 devices in a mesh: seq: 2 (over x), fsdp: 16 (over z, y, core).
Axes of the slice: x: 2, y: 2, z: 4, core: 2. Of those that a mesh axis runs over, the one named last changes fastest.
Arguments:
- signal: bfloat16 [16, 64, 20, 256], P('fsdp', None, 'seq'), may hold values from -20 to 20
- conv_weight: bfloat16 [256, 2048], P(None, 'fsdp')
- conv_bias: bfloat16 [2048], P('fsdp'), may hold values from -3 to 3
- ln_gain: bfloat16 [2048], P('fsdp'), may hold values from 0.099609375 to 1.8984375
- ln_bias: bfloat16 [2048], P('fsdp'), may hold values from -3 to 3
- w_space: bfloat16 [1024, 3072], P('fsdp')
- w_time: bfloat16 [1024, 3072], P('fsdp')
- w_out: bfloat16 [2048, 2048], P('fsdp'), may hold values from -0.125 to 0.125
Outputs:
- mixed: bfloat16 [16, 64, 20, 2048], P('fsdp', None, 'seq')
All inputs are finite; a program needn't handle non-finite values.
Results may differ from a plain program's by a relative error of at most 0.0054.
Values may be sent and summed in bfloat16 or wider, within the bound.
A program may use at most 128 MiB of HBM per device.

v0:
```python
import math

import jax
import jax.numpy as jnp
from jax import lax
from jax.sharding import PartitionSpec as P

HEADS = 16


def layer_norm(values, gain, shift):
    mean = jnp.mean(values, axis=-1, keepdims=True)
    centred = values - mean
    variance = jnp.mean(centred * centred, axis=-1, keepdims=True)
    return centred * lax.rsqrt(variance + 1e-05) * gain.astype(jnp.float32) + shift.astype(
        jnp.float32
    )


def attend(queries, keys_in, values_in):
    scale = 1.0 / math.sqrt(queries.shape[-1])
    scores = (
        jnp.einsum("bqhd,bkhd->bhqk", queries, keys_in, preferred_element_type=jnp.float32) * scale
    )
    highest = jnp.max(scores, axis=-1, keepdims=True)
    expo = jnp.exp(scores - highest)
    probs = (expo / jnp.sum(expo, axis=-1, keepdims=True)).astype(jnp.bfloat16)
    result = jnp.einsum("bhqk,bkhd->bqhd", probs, values_in, preferred_element_type=jnp.float32)
    return result.astype(jnp.bfloat16)


def project(features, weight):
    return jnp.dot(
        features,
        lax.all_gather(weight, "fsdp", axis=0, tiled=True),
        preferred_element_type=jnp.float32,
    )


def per_device(signal, conv_weight, conv_bias, ln_gain, ln_bias, w_space, w_time, w_out):
    kernel, bias_full, gain_full, shift_full = (
        lax.all_gather(conv_weight, "fsdp", axis=1, tiled=True),
        lax.all_gather(conv_bias, "fsdp", axis=0, tiled=True),
        lax.all_gather(ln_gain, "fsdp", axis=0, tiled=True),
        lax.all_gather(ln_bias, "fsdp", axis=0, tiled=True),
    )
    nights, channels, patch_count, samples = signal.shape
    model_width = kernel.shape[1]
    half_width = model_width // 2
    head_count = HEADS // 2
    head_size = half_width // head_count
    flat = signal.reshape(-1, samples)
    embed = (
        jnp.dot(flat, kernel, preferred_element_type=jnp.float32) + bias_full.astype(jnp.float32)
    ).astype(jnp.bfloat16)
    embed = lax.optimization_barrier(embed)
    normed = layer_norm(embed.astype(jnp.float32), gain_full, shift_full).astype(jnp.bfloat16)
    space_qkv = project(normed[:, :half_width], w_space).astype(jnp.bfloat16)
    space_qkv = space_qkv.reshape(channels, patch_count, 3, head_count, head_size).transpose(
        1, 0, 2, 3, 4
    )
    space_out = attend(space_qkv[:, :, 0], space_qkv[:, :, 1], space_qkv[:, :, 2])
    space_out = space_out.transpose(1, 0, 2, 3).reshape(-1, half_width)
    time_qkv = project(normed[:, half_width:], w_time).astype(jnp.bfloat16)
    time_qkv = time_qkv.reshape(channels, patch_count, 3, head_count, head_size)
    local_out = attend(
        lax.all_to_all(time_qkv[:, :, 0], "seq", split_axis=0, concat_axis=1, tiled=True),
        lax.all_to_all(time_qkv[:, :, 1], "seq", split_axis=0, concat_axis=1, tiled=True),
        lax.all_to_all(time_qkv[:, :, 2], "seq", split_axis=0, concat_axis=1, tiled=True),
    )
    time_out = lax.all_to_all(local_out, "seq", split_axis=1, concat_axis=0, tiled=True)
    joined = jnp.concatenate([space_out, time_out.reshape(-1, half_width)], axis=1)
    mixed = embed.astype(jnp.float32) + project(joined, w_out)
    return mixed.astype(jnp.bfloat16).reshape(nights, channels, patch_count, model_width)


def solution(mesh):
    in_specs = (
        P("fsdp", None, "seq", None),
        P(None, "fsdp"),
        P("fsdp"),
        P("fsdp"),
        P("fsdp"),
        P("fsdp", None),
        P("fsdp", None),
        P("fsdp", None),
    )
    out_specs = P("fsdp", None, "seq", None)
    return jax.shard_map(
        per_device, mesh=mesh, in_specs=in_specs, out_specs=out_specs, check_vma=False
    )
```

profile of v0, /device:TPU:6, one launch (start us, length us, event | category | flops | bytes accessed | tf_op | source)
XLA Modules:
  0.0 276.2 jit_solution(5845581829192867395)
XLA Ops:
  9.3 1.2 copy.44
  10.6 17.8 %all-gather = bf16[16,1,128]{2,1,0:T(2,128)(2,1)S(1)} all-gather(bf16[1,1,128]{2,1,0:T(2,128)(2,1)S(1)} %bitcast.84), channel_id=1, replica_groups=mesh['seq'=2,'fsdp'=16] {'fsdp'}, dimensions={0}, use_global_device_ids=true | all-gather | bytes 4352 | tf_op jit(solution)/shard_map/all_gather | solution.py:43
  28.5 21.2 %all-gather.1 = bf16[16,1,128]{2,1,0:T(2,128)(2,1)S(1)} all-gather(bf16[1,1,128]{2,1,0:T(2,128)(2,1)S(1)} %bitcast.85), channel_id=1, replica_groups=mesh['seq'=2,'fsdp'=16] {'fsdp'}, dimensions={0}, use_global_device_ids=true | all-gather | bytes 4352 | tf_op jit(solution)/shard_map/all_gather | solution.py:44
  49.7 17.3 %all-gather.2 = bf16[16,1,128]{2,1,0:T(2,128)(2,1)S(1)} all-gather(bf16[1,1,128]{2,1,0:T(2,128)(2,1)S(1)} %bitcast.86), channel_id=1, replica_groups=mesh['seq'=2,'fsdp'=16] {'fsdp'}, dimensions={0}, use_global_device_ids=true | all-gather | bytes 4352 | tf_op jit(solution)/shard_map/all_gather | solution.py:45
  67.1 2.1 add_convert_fusion
  70.4 2.5 fusion.7
  72.9 37.4 %all-gather.12.cloned.1.call-done = bf16[1024,3072]{1,0:T(8,128)(2,1)} async-done(((bf16[64,3072]{1,0:T(8,128)(2,1)}), bf16[1024,3072]{1,0:T(8,128)(2,1)}) %all-gather.12.cloned.1.call-update) | async-done | bytes 6291472 | tf_op jit(solution)/shard_map/all_gather | solution.py:35
  110.3 7.4 %fusion.19 = bf16[80,8,24,128]{3,1,2,0:T(8,128)(2,1)S(1)} fusion(bf16[1024,3072]{1,0:T(8,128)(2,1)} %all-gather.12.cloned.1.call-done, bf16[640,2048]{1,0:T(8,128)(2,1)} %fusion.7), kind=kOutput, calls=%fused_computation.28 | convolution fusion | flops 4028497920 | bytes 11534336 | tf_op jit(solution)/shard_map/dot_general | solution.py:33
  117.7 1.1 copy.70
  118.9 1.8 slice_bitcast_fusion.2
  120.6 19.2 %all_to_all.69 = bf16[64,10,8,128]{3,2,1,0:T(8,128)(2,1)} all-to-all(bf16[64,10,8,128]{3,2,1,0:T(8,128)(2,1)S(1)} %get-tuple-element.6), channel_id=1, replica_groups=mesh['seq'=2,'fsdp'=16] {'seq'}, dimensions={0} | all-to-all | bytes 2621440 | tf_op jit(solution)/shard_map/all_to_all | solution.py:67
  139.8 19.5 %all_to_all.70 = bf16[64,10,8,128]{3,2,1,0:T(8,128)(2,1)} all-to-all(bf16[64,10,8,128]{3,2,1,0:T(8,128)(2,1)S(1)} %get-tuple-element.7), channel_id=1, replica_groups=mesh['seq'=2,'fsdp'=16] {'seq'}, dimensions={0} | all-to-all | bytes 2621440 | tf_op jit(solution)/shard_map/all_to_all | solution.py:68
  159.4 6.2 %all-to-all-start = ((bf16[64,10,8,128]{3,2,1,0:T(8,128)(2,1)}), bf16[64,10,8,128]{3,2,1,0:T(8,128)(2,1)}, u32[]{:S(2)}, u32[]{:S(2)}) async-start(bf16[64,10,8,128]{3,2,1,0:T(8,128)(2,1)} %get-tuple-element.5), calls=%async_computation | async-start | bytes 2621440 | tf_op jit(solution)/shard_map/all_to_all | solution.py:69
  165.6 7.4 %all-gather.10.cloned.1.call-done = bf16[1024,3072]{1,0:T(8,128)(2,1)} async-done(((bf16[64,3072]{1,0:T(8,128)(2,1)}), bf16[1024,3072]{1,0:T(8,128)(2,1)}) %all-gather.10.cloned.1.call-update) | async-done | bytes 6291472 | tf_op jit(solution)/shard_map/all_gather | solution.py:35
  173.1 7.4 %fusion.18 = bf16[80,8,24,128]{3,1,2,0:T(8,128)(2,1)S(1)} fusion(bf16[1024,3072]{1,0:T(8,128)(2,1)} %all-gather.10.cloned.1.call-done, bf16[640,2048]{1,0:T(8,128)(2,1)} %fusion.7), kind=kOutput, calls=%fused_computation.27 | convolution fusion | flops 4028497920 | bytes 11534336 | tf_op jit(solution)/shard_map/dot_general | solution.py:33
  182.7 2.3 fusion.31
  185.4 1.2 copy.51
  187.2 1.2 copy.53
  188.4 1.6 copy.49
  191.5 8.9 %fusion.38 = (f32[32,8,20]{2,1,0:T(8,128)S(1)}, f32[32,8,20,20]{2,3,1,0:T(8,128)S(1)}) fusion(f32[32,8,20,20]{2,3,1,0:T(8,128)S(1)} %fusion.21), kind=kOutput, calls=%fused_computation.57 | output fusion | flops 409619 | bytes 839680 | tf_op jit(solution)/shard_map/sub | solution.py:26
  201.5 1.3 copy.58
  202.8 5.1 %all-to-all-start.3 = ((bf16[32,20,8,128]{3,2,0,1:T(8,128)(2,1)}), bf16[32,20,8,128]{3,2,0,1:T(8,128)(2,1)}, u32[]{:S(2)}, u32[]{:S(2)}) async-start(bf16[32,20,8,128]{3,2,0,1:T(8,128)(2,1)} %copy.58), calls=%async_computation.3 | async-start | bytes 2621440 | tf_op jit(solution)/shard_map/all_to_all | solution.py:71
  207.9 4.4 %fusion.39 = (f32[10,8,64]{2,1,0:T(8,128)S(1)}, f32[10,8,64,64]{2,3,1,0:T(8,128)S(1)}) fusion(f32[10,8,64,64]{2,3,1,0:T(8,128)} %fusion.31), kind=kOutput, calls=%fused_computation.58 | output fusion | flops 1310783 | bytes 2641920 | tf_op jit(solution)/shard_map/sub | solution.py:26
  212.3 2.0 fusion.29
  214.2 1.9 copy.47
  216.1 7.5 %all-to-all-done.3 = bf16[32,20,8,128]{3,2,0,1:T(8,128)(2,1)} async-done(((bf16[32,20,8,128]{3,2,0,1:T(8,128)(2,1)}), bf16[32,20,8,128]{3,2,0,1:T(8,128)(2,1)}, u32[]{:S(2)}, u32[]{:S(2)}) %all-to-all-start.3) | async-done | bytes 1310752 | tf_op jit(solution)/shard_map/all_to_all | solution.py:71
  223.6 1.6 copy.60
  225.3 2.3 copy_bitcast_fusion.1
  227.6 21.0 %all-gather.14.cloned.1.call-done = bf16[2048,2048]{1,0:T(8,128)(2,1)} async-done(((bf16[128,2048]{1,0:T(8,128)(2,1)}), bf16[2048,2048]{1,0:T(8,128)(2,1)}) %all-gather.14.cloned.1.call-update) | async-done | bytes 8388624 | tf_op jit(solution)/shard_map/all_gather | solution.py:35
  248.6 10.6 %fusion.8 = bf16[640,2048]{1,0:T(8,128)(2,1)} fusion(bf16[640,2048]{1,0:T(8,128)(2,1)S(1)} %add_convert_fusion, bf16[2048,2048]{1,0:T(8,128)(2,1)} %all-gather.14.cloned.1.call-done, bf16[640,1024]{1,0:T(8,128)(2,1)} %get-tuple-element.12, bf16[640,1024]{1,0:T(8,128)(2,1)} %get-tuple-element.13), kind=kOutput, calls=%fused_computation.11 | convolution fusion | flops 5377884160 | bytes 16252928 | tf_op jit(solution)/shard_map/dot_general | solution.py:33
  259.2 5.3 %reshape.43 = bf16[1,64,10,2048]{3,2,1,0:T(8,128)(2,1)} reshape(bf16[640,2048]{1,0:T(8,128)(2,1)} %fusion.8) | data formatting | bytes 5242880 | tf_op jit(solution)/shard_map/reshape | solution.py:74
  264.6 5.1 %copy.61 = bf16[1,64,10,2048]{3,1,2,0:T(8,128)(2,1)} copy(bf16[1,64,10,2048]{3,2,1,0:T(8,128)(2,1)} %reshape.43) | data formatting | bytes 5242880 | tf_op jit(solution)/shard_map/reshape | solution.py:74
  (40 shorter events, 9.9 us)
Async XLA Ops:
  6.5 4.1 %copy-start.6 = (bf16[128]{0:T(256)(128)(2,1)S(1)}, bf16[128]{0:T(256)(128)(2,1)}, u32[]{:S(2)}) copy-start(bf16[128]{0:T(256)(128)(2,1)} %param.10) | copy-start | bytes 772
  6.5 21.9 %copy-start.7 = (bf16[128]{0:T(256)(128)(2,1)S(1)}, bf16[128]{0:T(256)(128)(2,1)}, u32[]{:S(2)}) copy-start(bf16[128]{0:T(256)(128)(2,1)} %param.11) | copy-start | bytes 772
  6.5 43.2 %copy-start.8 = (bf16[128]{0:T(256)(128)(2,1)S(1)}, bf16[128]{0:T(256)(128)(2,1)}, u32[]{:S(2)}) copy-start(bf16[128]{0:T(256)(128)(2,1)} %param.12) | copy-start | bytes 772
  6.5 60.5 %all-gather.8.cloned.1.call-start = ((), (), s32[]{:S(2)}) async-start(), calls=%async_computation.4 | async-start | bytes 1114112 | tf_op jit(solution)/shard_map/all_gather | solution.py:42
  7.3 103.0 %all-gather.12.cloned.1.call-start = ((), (), s32[]{:S(2)}) async-start(), calls=%async_computation.6 | async-start | bytes 6684672 | tf_op jit(solution)/shard_map/all_gather | solution.py:35
  8.0 165.0 %all-gather.10.cloned.1.call-start = ((), (), s32[]{:S(2)}) async-start(), calls=%async_computation.5 | async-start | bytes 6684672 | tf_op jit(solution)/shard_map/all_gather | solution.py:35
  8.7 239.9 %all-gather.14.cloned.1.call-start = ((), (), s32[]{:S(2)}) async-start(), calls=%async_computation.7 | async-start | bytes 8912896 | tf_op jit(solution)/shard_map/all_gather | solution.py:35
  159.4 29.0 %all-to-all-start = ((bf16[64,10,8,128]{3,2,1,0:T(8,128)(2,1)}), bf16[64,10,8,128]{3,2,1,0:T(8,128)(2,1)}, u32[]{:S(2)}, u32[]{:S(2)}) async-start(bf16[64,10,8,128]{3,2,1,0:T(8,128)(2,1)} %get-tuple-element.5), calls=%async_computation | async-start | bytes 2621440 | tf_op jit(solution)/shard_map/all_to_all | solution.py:69
  182.7 2.7 copy-start
  182.7 2.7 copy-start.4
  185.4 1.8 copy-start.5
  188.4 1.7 copy-start.1
  188.4 2.1 copy-start.2
  202.8 20.8 %all-to-all-start.3 = ((bf16[32,20,8,128]{3,2,0,1:T(8,128)(2,1)}), bf16[32,20,8,128]{3,2,0,1:T(8,128)(2,1)}, u32[]{:S(2)}, u32[]{:S(2)}) async-start(bf16[32,20,8,128]{3,2,0,1:T(8,128)(2,1)} %copy.58), calls=%async_computation.3 | async-start | bytes 2621440 | tf_op jit(solution)/shard_map/all_to_all | solution.py:71
  223.6 1.7 copy-start.3
Sparse Core Ops, SparseCore 0:
  9.5 37.8 all-gather.7
  49.7 60.5 all-gather.11
  112.6 60.4 all-gather.9
  175.1 73.4 all-gather.13
where the time goes:
time: 279 us; the launch traced here: 276 us
  blocking collectives  95.1 us (34%)
  waiting for transfers between devices  75.9 us (27%)
  matrix products  33.8 us (12%)
  local copies, waits for them, and re-layouts  29.6 us (11%)
  other arithmetic  17.1 us (6%)
  between operations  13.3 us (5%)
  starting transfers between devices  11.4 us (4%)
    all_gather x3, waiting for transfers between devices, project(): lax.all_gather(weight, 'fsdp', axis=0, tiled=True)  65.8 us
    dot_general x3, matrix products, project(): jnp.dot(features, lax.all_gather(weight, 'fsdp', axis=0, tiled=True), pre...  25.5 us
    all_gather x1, blocking collectives, per_device(): lax.all_gather(ln_gain, 'fsdp', axis=0, tiled=True)  21.2 us
    all_to_all x1, blocking collectives, per_device(): lax.all_to_all(time_qkv[:, :, 1], 'seq', split_axis=0, concat_axis=1, til...  19.5 us
    all_to_all x1, blocking collectives, per_device(): lax.all_to_all(time_qkv[:, :, 0], 'seq', split_axis=0, concat_axis=1, til...  19.2 us
    all_gather x1, blocking collectives, per_device(): lax.all_gather(conv_bias, 'fsdp', axis=0, tiled=True)  17.8 us
    all_gather x1, blocking collectives, per_device(): lax.all_gather(ln_bias, 'fsdp', axis=0, tiled=True)  17.3 us
    sub x2, other arithmetic, attend(): expo = jnp.exp(scores - highest)  13.3 us
  transfers between devices with their start and end apart: 6, of which 4 were waited for; matrix products, arithmetic and copies ran while one was open for 21% of the time, Pallas kernels for 0%

commit v1 on v0

--- a/solution.py
+++ b/solution.py
@@ -2,10 +2,15 @@
 
 import jax
 import jax.numpy as jnp
+import ml_dtypes
+import numpy as np
 from jax import lax
+from jax.experimental import pallas as pl
+from jax.experimental.pallas import tpu as pltpu
 from jax.sharding import PartitionSpec as P
 
 HEADS = 16
+MESH = pl.DeviceIdType.MESH
 
 
 def layer_norm(values, gain, shift):
@@ -74,6 +79,352 @@
     return mixed.astype(jnp.bfloat16).reshape(nights, channels, patch_count, model_width)
 
 
+RING = 8
+CONV, PROJ, OUT = 0, 1, 2
+
+
+def shard_at(position, core):
+    position = lax.rem(position + 2 * RING, RING)
+    y = position // 4
+    z = jnp.where(y == 0, position, 7 - position)
+    return (z * 2 + y) * 2 + core
+
+
+ROWS = 160
+
+
+def night_kernel(
+    sig_ref, conv_ref, space_ref, time_ref, out_ref, to_role_ref, to_own_ref, mask_a_ref, mask_b_ref,
+    mixed_ref,
+    sig_full, sig_role, conv_full, proj_full, out_full, normed, qkv, result, outgoing, joined, total,
+    ring_send, ring_recv, sib_send, sib_recv, x_send, x_recv, sibx_send, sibx_recv, own_sem, sig_sem,
+    swap_send, swap_recv,
+):
+    s = lax.axis_index("seq")
+    f = lax.axis_index("fsdp")
+    core = lax.rem(f, 2)
+    chip = f // 2
+    y = lax.rem(chip, 2)
+    z = chip // 2
+    r = jnp.where(y == 0, z, 7 - z)
+    d = 1 - 2 * core
+    ahead = {"seq": s, "fsdp": shard_at(r + d, core)}
+    behind = {"seq": s, "fsdp": shard_at(r - d, core)}
+    sibling = {"seq": s, "fsdp": f + d}
+    across = {"seq": 1 - s, "fsdp": f}
+    depth, width = out_ref.shape
+    half = width // 2
+    cols = conv_ref.shape[1]
+    proj_depth = space_ref.shape[0]
+    tokens, samples = sig_ref.shape
+    quarter = depth // 4
+    head_size = width // HEADS
+    pair = 2 * head_size
+
+    def place(kind, shard):
+        if kind == CONV:
+            return conv_full.at[:, pl.ds(pl.multiple_of(shard * cols, cols), cols)]
+        if kind == PROJ:
+            return proj_full.at[pl.ds(pl.multiple_of(shard * proj_depth, proj_depth), proj_depth)]
+        start = pl.multiple_of(shard * depth + s * quarter, quarter)
+        return out_full.at[pl.ds(start, 3 * quarter)]
+
+    def place_x(shard, side):
+        start = pl.multiple_of(shard * depth + side * 3 * quarter, quarter)
+        return out_full.at[pl.ds(start, quarter)]
+
+    def shard_of(k, c, direction):
+        if k <= 4:
+            return shard_at(r - k * direction, c)
+        return shard_at(r + (k - 4) * direction, c)
+
+    own_conv = pltpu.make_async_copy(conv_ref, place(CONV, f), own_sem.at[0])
+    own_proj_a = pltpu.make_async_copy(space_ref, place(PROJ, f), own_sem.at[1])
+    own_proj_b = pltpu.make_async_copy(time_ref, place(PROJ, f), own_sem.at[1])
+    own_rows = pl.ds(pl.multiple_of(f * depth, depth), depth)
+    own_out = pltpu.make_async_copy(out_ref, out_full.at[own_rows], own_sem.at[2])
+    own_conv.start()
+    pl.when(s == 0)(own_proj_a.start)
+    pl.when(s == 1)(own_proj_b.start)
+    own_out.start()
+
+    barrier = pltpu.get_barrier_semaphore()
+    for other in (ahead, behind, sibling, across):
+        pl.semaphore_signal(barrier, inc=1, device_id=other, device_id_type=MESH)
+    pl.semaphore_wait(barrier, 4)
+
+    sent = []
+
+    def send(src, dst, send_sem, recv_sem, device):
+        copy = pltpu.make_async_remote_copy(
+            src_ref=src, dst_ref=dst, send_sem=send_sem, recv_sem=recv_sem,
+            device_id=device, device_id_type=MESH,
+        )
+        copy.start()
+        sent.append(copy)
+
+    def arrive(dst, recv_sem):
+        pltpu.make_async_remote_copy(
+            src_ref=dst, dst_ref=dst, send_sem=recv_sem, recv_sem=recv_sem,
+            device_id=sibling, device_id_type=MESH,
+        ).wait_recv()
+
+    def onward(kind, k):
+        shard = shard_of(k, core, d)
+        dst = place(kind, shard)
+        if k < 4:
+            send(dst, dst, ring_send.at[kind, k + 1], ring_recv.at[kind, k + 1], ahead)
+        if k == 0 or 5 <= k < 7:
+            nxt = 5 if k == 0 else k + 1
+            send(dst, dst, ring_send.at[kind, nxt], ring_recv.at[kind, nxt], behind)
+        if kind == OUT and k == 0:
+            quart = place_x(shard, 1 - s)
+            send(quart, quart, sibx_send.at[0], sibx_recv.at[0], sibling)
+        elif kind == OUT:
+            quart = place_x(shard, s)
+            send(quart, quart, x_send.at[k], x_recv.at[k], across)
+        send(dst, dst, sib_send.at[kind, k], sib_recv.at[kind, k], sibling)
+
+    both = ((1, 5), (2, 6), (3, 7), (4,))
+
+    def step(kind, at):
+        for k in both[at]:
+            arrive(place(kind, shard_of(k, core, d)), ring_recv.at[kind, k])
+            onward(kind, k)
+
+    def step_x(*slots):
+        for k in slots:
+            dst = place_x(shard_of(k, core, d), 1 - s)
+            arrive(dst, x_recv.at[k])
+            send(dst, dst, sibx_send.at[k], sibx_recv.at[k], sibling)
+
+    def from_sibling(kind, k):
+        arrive(place(kind, shard_of(k, 1 - core, -d)), sib_recv.at[kind, k])
+
+    def embed(x):
+        e = jnp.dot(x, conv_full[:samples], preferred_element_type=jnp.float32)
+        return (e + conv_full[samples : samples + 1].astype(jnp.float32)).astype(jnp.bfloat16)
+
+    def norm_rows(first, count):
+        @pl.loop(first, first + count)
+        def _(i):
+            rows = pl.ds(pl.multiple_of(i * ROWS, ROWS), ROWS)
+            e = embed(sig_role[rows]).astype(jnp.float32)
+            mean = jnp.mean(e, axis=-1, keepdims=True)
+            centred = e - mean
+            variance = jnp.mean(centred * centred, axis=-1, keepdims=True)
+            inverse = lax.rsqrt(variance + 1e-05)
+
+            def keep(lo):
+                part = slice(lo, lo + half)
+                gain = conv_full[samples + 1 : samples + 2, part].astype(jnp.float32)
+                shift = conv_full[samples + 2 : samples + 3, part].astype(jnp.float32)
+                normed[rows] = (centred[:, part] * inverse * gain + shift).astype(jnp.bfloat16)
+
+            pl.when(s == 0)(lambda: keep(0))
+            pl.when(s == 1)(lambda: keep(half))
+
+    def start_total():
+        @pl.loop(0, tokens // ROWS)
+        def _(i):
+            rows = pl.ds(pl.multiple_of(i * ROWS, ROWS), ROWS)
+            total[rows] = embed(sig_ref[rows]).astype(jnp.float32)
+
+    def attend_rows(q, k, v, allowed):
+        scores = lax.dot_general(
+            q, k, (((1,), (1,)), ((), ())), preferred_element_type=jnp.float32
+        ) * (1.0 / math.sqrt(head_size))
+        scores = jnp.where(allowed, scores, -jnp.inf)
+        highest = jnp.max(scores, axis=-1, keepdims=True)
+        expo = jnp.exp(scores - highest)
+        probs = (expo / jnp.sum(expo, axis=-1, keepdims=True)).astype(jnp.bfloat16)
+        return jnp.dot(probs, v, preferred_element_type=jnp.float32).astype(jnp.bfloat16)
+
+    def heads(j):
+        @pl.loop(0, 2 * tokens // (2 * ROWS))
+        def _(i):
+            rows = pl.ds(pl.multiple_of(i * 2 * ROWS, 2 * ROWS), 2 * ROWS)
+            for part in range(3):
+                w = proj_full[:, part * half + j * pair : part * half + (j + 1) * pair]
+                value = jnp.dot(normed[rows], w, preferred_element_type=jnp.float32)
+                qkv[rows, part * pair : (part + 1) * pair] = value.astype(jnp.bfloat16)
+
+        at = slice(j * pair, (j + 1) * pair)
+
+        @pl.when(s == 0)
+        def _():
+            count = mask_a_ref.shape[0]
+
+            @pl.loop(0, 2 * tokens // count)
+            def _(g):
+                rows = pl.ds(pl.multiple_of(g * count, count), count)
+                allowed = mask_a_ref[...] > 0
+                for h in range(2):
+                    q, k, v = (
+                        qkv[rows, part * pair + h * head_size : part * pair + (h + 1) * head_size]
+                        for part in range(3)
+                    )
+                    to = j * pair + h * head_size
+                    result[rows, to : to + head_size] = attend_rows(q, k, v, allowed)
+
+        @pl.when(s == 1)
+        def _():
+            count = mask_b_ref.shape[0] // 2
+
+            @pl.loop(0, tokens // count)
+            def _(g):
+                first = pl.ds(pl.multiple_of(g * count, 16), count)
+                second = pl.ds(pl.multiple_of(tokens + g * count, 16), count)
+                allowed = mask_b_ref[...] > 0
+                for h in range(2):
+                    q, k, v = (
+                        jnp.concatenate(
+                            [
+                                qkv[rows, part * pair + h * head_size : part * pair + (h + 1) * head_size]
+                                for rows in (first, second)
+                            ],
+                            axis=0,
+                        )
+                        for part in range(3)
+                    )
+                    to = j * pair + h * head_size
+                    value = attend_rows(q, k, v, allowed)
+                    result[first, to : to + head_size] = value[:count]
+                    result[second, to : to + head_size] = value[count:]
+
+        mine = pl.ds(pl.multiple_of(s * half + j * pair, pair), pair)
+
+        def reorder(side):
+            rows = pl.ds(pl.multiple_of(side * tokens, tokens), tokens)
+            return jnp.dot(
+                to_own_ref[...], result[rows, at], preferred_element_type=jnp.float32
+            ).astype(jnp.bfloat16)
+
+        outgoing[:, at] = reorder(1 - s)
+        send(outgoing.at[:, at], joined.at[:, mine], swap_send.at[j], swap_recv.at[j], across)
+        joined[:, mine] = reorder(s)
+
+    def add_chip(k, last=False):
+        at = pl.ds(pl.multiple_of((shard_of(k, core, d) // 2) * 2 * depth, 2 * depth), 2 * depth)
+
+        @pl.loop(0, tokens // ROWS)
+        def _(i):
+            rows = pl.ds(pl.multiple_of(i * ROWS, ROWS), ROWS)
+            value = total[rows] + jnp.dot(
+                joined[rows, at], out_full[at, :], preferred_element_type=jnp.float32
+            )
+            if last:
+                mixed_ref[rows] = value.astype(jnp.bfloat16)
+            else:
+                total[rows] = value
+
+    send(sig_ref, sig_full.at[s], sig_sem.at[0], sig_sem.at[1], across)
+    own_conv.wait()
+    onward(CONV, 0)
+    pl.when(s == 0)(own_proj_a.wait)
+    pl.when(s == 1)(own_proj_b.wait)
+    onward(PROJ, 0)
+    own_out.wait()
+    step(CONV, 0)
+    step(CONV, 1)
+    sig_full[s] = sig_ref[...]
+    step(CONV, 2)
+    step(CONV, 3)
+    step(PROJ, 0)
+    onward(OUT, 0)
+    arrive(sig_full.at[1 - s], sig_sem.at[1])
+    for side in range(2):
+        sig_role[side * tokens : (side + 1) * tokens] = jnp.dot(
+            to_role_ref[...], sig_full[side], preferred_element_type=jnp.float32
+        ).astype(jnp.bfloat16)
+    for k in range(RING):
+        from_sibling(CONV, k)
+    norm_rows(0, 3)
+    step(PROJ, 1)
+    norm_rows(3, 3)
+    step(PROJ, 2)
+    step(OUT, 0)
+    norm_rows(6, 2)
+    start_total()
+    step(PROJ, 3)
+    step(OUT, 1)
+    step_x(1, 5)
+    for k in range(RING):
+        from_sibling(PROJ, k)
+    heads(0)
+    step(OUT, 2)
+    step_x(2, 6)
+    heads(1)
+    step(OUT, 3)
+    step_x(3, 7)
+    heads(2)
+    step_x(4)
+    heads(3)
+    for j in range(HEADS // 4):
+        theirs = pl.ds(pl.multiple_of((1 - s) * half + j * pair, pair), pair)
+        arrive(joined.at[:, theirs], swap_recv.at[j])
+    slots = (0, 1, 5, 2, 6, 3, 7, 4)
+    partner = {0: 0, 1: 5, 5: 1, 2: 6, 6: 2, 3: 7, 7: 3, 4: 4}
+    for k in slots:
+        from_sibling(OUT, partner[k])
+        arrive(place_x(shard_of(partner[k], 1 - core, -d), 1 - s), sibx_recv.at[partner[k]])
+        add_chip(k, last=k == 4)
+    for copy in sent:
+        copy.wait_send()
+
+
+def split_by_branch(signal, conv_weight, conv_bias, ln_gain, ln_bias, w_space, w_time, w_out):
+    s = lax.axis_index("seq")
+    _, channels, patches, samples = signal.shape
+    width = w_out.shape[1]
+    half = width // 2
+    tokens = channels * patches
+    shards = 2 * RING
+    rows = jnp.stack([conv_bias, ln_gain, ln_bias])
+    conv = jnp.concatenate([conv_weight, jnp.pad(rows, ((0, 13), (0, 0)))], axis=0)
+    order = np.arange(tokens).reshape(channels, patches)
+    natural = np.eye(tokens, dtype=ml_dtypes.bfloat16)
+    patch_major = natural[order.T.reshape(-1)]
+    to_role = jnp.where(s == 0, jnp.asarray(patch_major), jnp.asarray(natural))
+    to_own = jnp.where(s == 0, jnp.asarray(patch_major.T), jnp.asarray(natural))
+    patch_of = np.arange(2 * channels) // channels
+    mask_a = (patch_of[:, None] == patch_of[None]).astype(np.float32)
+    channel_of = np.tile(np.arange(8 * patches) // patches, 2)
+    mask_b = (channel_of[:, None] == channel_of[None]).astype(np.float32)
+    dma = pltpu.SemaphoreType.DMA
+    vmem = pl.BlockSpec(memory_space=pltpu.VMEM)
+    anywhere = pl.BlockSpec(memory_space=pl.ANY)
+    bf16 = jnp.bfloat16
+    flops = 4 * tokens * (width * samples + half * 3 * half + width * width // 2)
+    mixed = pl.pallas_call(
+        night_kernel,
+        out_shape=jax.ShapeDtypeStruct((tokens, width), bf16),
+        in_specs=[vmem, anywhere, anywhere, anywhere, anywhere, vmem, vmem, vmem, vmem],
+        out_specs=vmem,
+        scratch_shapes=[
+            pltpu.VMEM((2, tokens, samples), bf16),
+            pltpu.VMEM((2 * tokens, samples), bf16),
+            pltpu.VMEM((conv.shape[0], width), bf16),
+            pltpu.VMEM((shards * w_space.shape[0], w_space.shape[1]), bf16),
+            pltpu.VMEM((shards * w_out.shape[0], width), bf16),
+            pltpu.VMEM((2 * tokens, half), bf16),
+            pltpu.VMEM((2 * tokens, 6 * width // HEADS), bf16),
+            pltpu.VMEM((2 * tokens, half), bf16),
+            pltpu.VMEM((tokens, half), bf16),
+            pltpu.VMEM((tokens, width), bf16),
+            pltpu.VMEM((tokens, width), jnp.float32),
+            dma((3, 8)), dma((3, 8)), dma((3, 8)), dma((3, 8)),
+            dma((8,)), dma((8,)), dma((8,)), dma((8,)), dma((3,)), dma((2,)), dma((4,)), dma((4,)),
+        ],
+        compiler_params=pltpu.CompilerParams(
+            collective_id=0, has_side_effects=True, vmem_limit_bytes=60 * 2**20
+        ),
+        cost_estimate=pl.CostEstimate(flops=flops, bytes_accessed=2**23, transcendentals=2**21),
+    )(signal.reshape(tokens, samples), conv, w_space, w_time, w_out, to_role, to_own,
+      jnp.asarray(mask_a), jnp.asarray(mask_b))
+    return mixed.reshape(1, channels, patches, width)
+
+
 def solution(mesh):
     in_specs = (
         P("fsdp", None, "seq", None),
@@ -86,6 +437,8 @@
         P("fsdp", None),
     )
     out_specs = P("fsdp", None, "seq", None)
+    whole_night = mesh.shape["seq"] == 2 and mesh.shape["fsdp"] == 2 * RING
+    body = split_by_branch if whole_night else per_device
     return jax.shard_map(
-        per_device, mesh=mesh, in_specs=in_specs, out_specs=out_specs, check_vma=False
-    )
+        body, mesh=mesh, in_specs=in_specs, out_specs=out_specs, check_vma=False
+    )

time: 279 us -> 150 us (0.54)
  Pallas kernels: 0 us -> 131 us
  blocking collectives: 95.1 us -> 0 us
  waiting for transfers between devices: 75.9 us -> 0 us
  matrix products: 33.8 us -> 0 us
  local copies, waits for them, and re-layouts: 29.6 us -> 12.5 us
  between operations: 13.3 us -> 0.02 us
  other arithmetic: 17.1 us -> 4.63 us
  starting transfers between devices: 11.4 us -> 0 us
    pallas_call x0 -> x1, Pallas kernels: none -> 131 us  [split_by_branch(): pl.pallas_call(night_kernel, out_shape=jax.ShapeDtypeStruct((tokens, widt...]
    all_gather x4 -> x0, waiting for transfers between devices: 65.9 us -> none  [the longest x3 65.8 us: project(): lax.all_gather(weight, 'fsdp', axis=0, tiled=True)]
    all_gather x3 -> x0, blocking collectives: 56.3 us -> none  [the longest x1 21.2 us: per_device(): lax.all_gather(ln_gain, 'fsdp', axis=0, tiled=True)]
    all_to_all x2 -> x0, blocking collectives: 38.7 us -> none  [the longest x1 19.5 us: per_device(): lax.all_to_all(time_qkv[:, :, 1], 'seq', split_axis=0, concat_axis=1, til...]
    dot_general x8 -> x0, matrix products: 33.8 us -> none  [the longest x3 25.5 us: project(): jnp.dot(features, lax.all_gather(weight, 'fsdp', axis=0, tiled=True), pre...]
    sub x2 -> x0, other arithmetic: 13.3 us -> none  [attend(): expo = jnp.exp(scores - highest)]
    all_to_all x2 -> x0, starting transfers between devices: 11.3 us -> none  [the longest x1 6.24 us: per_device(): lax.all_to_all(time_qkv[:, :, 2], 'seq', split_axis=0, concat_axis=1, til...]
    all_to_all x2 -> x0, waiting for transfers between devices: 7.46 us -> none  [the longest x1 7.46 us: per_device(): lax.all_to_all(local_out, 'seq', split_axis=1, concat_axis=0, tiled=True)]
  transfers between devices with their start and end apart: 6 -> 0, of which waited for: 4 -> 0; matrix products, arithmetic and copies ran while one was open for 21% -> 0% of each run, Pallas kernels for 0% -> 0%
where the time goes in v1:
time: 150 us; the launch traced here: 148 us
  Pallas kernels  131 us (87%)
  local copies, waits for them, and re-layouts  12.5 us (8%)
  other arithmetic  4.63 us (3%)
    pallas_call x1, Pallas kernels, split_by_branch(): pl.pallas_call(night_kernel, out_shape=jax.ShapeDtypeStruct((tokens, widt...  131 us
    reshape x2, local copies, waits for them, and re-layouts, split_by_branch(): return mixed.reshape(1, channels, patches, width)  10.5 us

profile of v1, /device:TPU:6, one launch (start us, length us, event | category | flops | bytes accessed | tf_op | source)
XLA Modules:
  0.0 148.0 jit_solution(16985898948232178682)
XLA Ops:
  0.0 0.7 fusion.4
  0.7 1.5 pad_maximum_fusion.conv_ref
  2.2 1.2 copy.16
  3.3 0.8 reshape.6.sig_ref
  4.2 2.5 %broadcast_select_fusion = (bf16[640,640]{1,0:T(8,128)(2,1)}, bf16[640,640]{1,0:T(8,128)(2,1)}) fusion(bf16[640,640]{1,0:T(8,128)(2,1)} %constant.22.clone, bf16[640,640]{1,0:T(8,128)(2,1)} %constant.21.clone, pred[]{:T(512)S(6)} %eq.4, bf16[640,640]{1,0:T(8,128)(2,1)} %constant.20.clone), kind=kLoop, calls=%fused_computation | loop fusion | flops 819200 | bytes 4096001 | tf_op jit(solution)/shard_map/jit(_where)/select_n | solution.py:389
  6.7 130.8 %shard_map.127 = bf16[640,2048]{1,0:T(8,128)(2,1)} custom-call(bf16[640,256]{1,0:T(8,128)(2,1)} %reshape.6.sig_ref, bf16[272,128]{1,0:T(8,128)(2,1)} %pad_maximum_fusion.conv_ref, bf16[64,3072]{1,0:T(8,128)(2,1)} %space_ref.1, bf16[64,3072]{1,0:T(8,128)(2,1)} %time_ref.1, bf16[128,2048]{1,0:T(8,128)(2,1)} %out_ref.1, ...), custom_call_target="tpu_custom_call" | custom-call | flops 14763950080 | bytes 8388608 | tf_op jit(solution)/shard_map/pallas_call | solution.py:399
  137.5 5.4 %reshape.7 = bf16[1,64,10,2048]{3,2,1,0:T(8,128)(2,1)} reshape(bf16[640,2048]{1,0:T(8,128)(2,1)} %shard_map.127) | data formatting | bytes 5242880 | tf_op jit(solution)/shard_map/reshape | solution.py:425
  142.9 5.1 %copy.17 = bf16[1,64,10,2048]{3,1,2,0:T(8,128)(2,1)} copy(bf16[1,64,10,2048]{3,2,1,0:T(8,128)(2,1)} %reshape.7) | data formatting | bytes 5242880 | tf_op jit(solution)/shard_map/reshape | solution.py:425

commit v2 on v1

--- a/solution.py
+++ b/solution.py
@@ -1,8 +1,8 @@
+import functools
 import math
 
 import jax
 import jax.numpy as jnp
-import ml_dtypes
 import numpy as np
 from jax import lax
 from jax.experimental import pallas as pl
@@ -80,7 +80,7 @@
 
 
 RING = 8
-CONV, PROJ, OUT = 0, 1, 2
+CONV, PROJ_A, PROJ_B, OUT_A, OUT_B = range(5)
 
 
 def shard_at(position, core):
@@ -94,9 +94,10 @@
 
 
 def night_kernel(
-    sig_ref, conv_ref, space_ref, time_ref, out_ref, to_role_ref, to_own_ref, mask_a_ref, mask_b_ref,
+    channels, patches, sig_ref, conv_ref, space_ref, time_ref, out_ref, mask_a_ref, mask_b_ref,
     mixed_ref,
     sig_full, sig_role, conv_full, proj_full, out_full, normed, qkv, result, outgoing, joined, total,
+    to_role_ref, to_own_ref,
     ring_send, ring_recv, sib_send, sib_recv, x_send, x_recv, sibx_send, sibx_recv, own_sem, sig_sem,
     swap_send, swap_recv,
 ):
@@ -124,10 +125,13 @@
     def place(kind, shard):
         if kind == CONV:
             return conv_full.at[:, pl.ds(pl.multiple_of(shard * cols, cols), cols)]
-        if kind == PROJ:
-            return proj_full.at[pl.ds(pl.multiple_of(shard * proj_depth, proj_depth), proj_depth)]
-        start = pl.multiple_of(shard * depth + s * quarter, quarter)
-        return out_full.at[pl.ds(start, 3 * quarter)]
+        if kind in (PROJ_A, PROJ_B):
+            count = proj_depth // 2
+            start = pl.multiple_of(shard * proj_depth + (kind - PROJ_A) * count, count)
+            return proj_full.at[pl.ds(start, count)]
+        count = 3 * depth // 8
+        first = s * (depth - count) if kind == OUT_A else count - s * (2 * count - 5 * depth // 8)
+        return out_full.at[pl.ds(pl.multiple_of(shard * depth + first, 16), count)]
 
     def place_x(shard, side):
         start = pl.multiple_of(shard * depth + side * 3 * quarter, quarter)
@@ -139,8 +143,9 @@
         return shard_at(r + (k - 4) * direction, c)
 
     own_conv = pltpu.make_async_copy(conv_ref, place(CONV, f), own_sem.at[0])
-    own_proj_a = pltpu.make_async_copy(space_ref, place(PROJ, f), own_sem.at[1])
-    own_proj_b = pltpu.make_async_copy(time_ref, place(PROJ, f), own_sem.at[1])
+    own_proj_rows = pl.ds(pl.multiple_of(f * proj_depth, proj_depth), proj_depth)
+    own_proj_a = pltpu.make_async_copy(space_ref, proj_full.at[own_proj_rows], own_sem.at[1])
+    own_proj_b = pltpu.make_async_copy(time_ref, proj_full.at[own_proj_rows], own_sem.at[1])
     own_rows = pl.ds(pl.multiple_of(f * depth, depth), depth)
     own_out = pltpu.make_async_copy(out_ref, out_full.at[own_rows], own_sem.at[2])
     own_conv.start()
@@ -177,10 +182,10 @@
         if k == 0 or 5 <= k < 7:
             nxt = 5 if k == 0 else k + 1
             send(dst, dst, ring_send.at[kind, nxt], ring_recv.at[kind, nxt], behind)
-        if kind == OUT and k == 0:
+        if kind == OUT_A and k == 0:
             quart = place_x(shard, 1 - s)
             send(quart, quart, sibx_send.at[0], sibx_recv.at[0], sibling)
-        elif kind == OUT:
+        elif kind == OUT_A:
             quart = place_x(shard, s)
             send(quart, quart, x_send.at[k], x_recv.at[k], across)
         send(dst, dst, sib_send.at[kind, k], sib_recv.at[kind, k], sibling)
@@ -200,6 +205,14 @@
 
     def from_sibling(kind, k):
         arrive(place(kind, shard_of(k, 1 - core, -d)), sib_recv.at[kind, k])
+
+    def set_orders():
+        row = lax.broadcasted_iota(jnp.int32, (tokens, 1), 0)
+        col = lax.broadcasted_iota(jnp.int32, (tokens, tokens), 1)
+        source = lax.rem(row, patches) * channels + lax.div(row, patches)
+        to_role_ref[...] = (jnp.where(s == 0, row, source) == col).astype(jnp.bfloat16)
+        target = lax.rem(row, channels) * patches + lax.div(row, channels)
+        to_own_ref[...] = (jnp.where(s == 0, row, target) == col).astype(jnp.bfloat16)
 
     def embed(x):
         e = jnp.dot(x, conv_full[:samples], preferred_element_type=jnp.float32)
@@ -240,7 +253,7 @@
         probs = (expo / jnp.sum(expo, axis=-1, keepdims=True)).astype(jnp.bfloat16)
         return jnp.dot(probs, v, preferred_element_type=jnp.float32).astype(jnp.bfloat16)
 
-    def heads(j):
+    def heads(j, between=lambda: None):
         @pl.loop(0, 2 * tokens // (2 * ROWS))
         def _(i):
             rows = pl.ds(pl.multiple_of(i * 2 * ROWS, 2 * ROWS), 2 * ROWS)
@@ -249,6 +262,7 @@
                 value = jnp.dot(normed[rows], w, preferred_element_type=jnp.float32)
                 qkv[rows, part * pair : (part + 1) * pair] = value.astype(jnp.bfloat16)
 
+        between()
         at = slice(j * pair, (j + 1) * pair)
 
         @pl.when(s == 0)
@@ -323,15 +337,18 @@
     onward(CONV, 0)
     pl.when(s == 0)(own_proj_a.wait)
     pl.when(s == 1)(own_proj_b.wait)
-    onward(PROJ, 0)
+    onward(PROJ_A, 0)
+    onward(PROJ_B, 0)
     own_out.wait()
+    set_orders()
     step(CONV, 0)
     step(CONV, 1)
     sig_full[s] = sig_ref[...]
+    step(PROJ_A, 0)
     step(CONV, 2)
+    step(PROJ_B, 0)
     step(CONV, 3)
-    step(PROJ, 0)
-    onward(OUT, 0)
+    onward(OUT_A, 0)
     arrive(sig_full.at[1 - s], sig_sem.at[1])
     for side in range(2):
         sig_role[side * tokens : (side + 1) * tokens] = jnp.dot(
@@ -339,26 +356,41 @@
         ).astype(jnp.bfloat16)
     for k in range(RING):
         from_sibling(CONV, k)
-    norm_rows(0, 3)
-    step(PROJ, 1)
-    norm_rows(3, 3)
-    step(PROJ, 2)
-    step(OUT, 0)
+    step(PROJ_A, 1)
+    norm_rows(0, 2)
+    step(PROJ_B, 1)
+    onward(OUT_B, 0)
+    norm_rows(2, 1)
+    step(OUT_A, 0)
+    norm_rows(3, 2)
+    step(PROJ_A, 2)
+    norm_rows(5, 1)
+    step(OUT_B, 0)
+    step(PROJ_B, 2)
     norm_rows(6, 2)
+    step(OUT_A, 1)
+    step(PROJ_A, 3)
+    step_x(1, 5)
     start_total()
-    step(PROJ, 3)
-    step(OUT, 1)
-    step_x(1, 5)
+    step(OUT_B, 1)
+    step(PROJ_B, 3)
     for k in range(RING):
-        from_sibling(PROJ, k)
-    heads(0)
-    step(OUT, 2)
-    step_x(2, 6)
-    heads(1)
-    step(OUT, 3)
-    step_x(3, 7)
-    heads(2)
-    step_x(4)
+        from_sibling(PROJ_A, k)
+        from_sibling(PROJ_B, k)
+
+    def second():
+        step(OUT_A, 2)
+        step_x(2, 6)
+        step(OUT_B, 2)
+
+    def third():
+        step(OUT_A, 3)
+        step_x(3, 7)
+        step(OUT_B, 3)
+
+    heads(0, second)
+    heads(1, third)
+    heads(2, lambda: step_x(4))
     heads(3)
     for j in range(HEADS // 4):
         theirs = pl.ds(pl.multiple_of((1 - s) * half + j * pair, pair), pair)
@@ -366,7 +398,8 @@
     slots = (0, 1, 5, 2, 6, 3, 7, 4)
     partner = {0: 0, 1: 5, 5: 1, 2: 6, 6: 2, 3: 7, 7: 3, 4: 4}
     for k in slots:
-        from_sibling(OUT, partner[k])
+        from_sibling(OUT_A, partner[k])
+        from_sibling(OUT_B, partner[k])
         arrive(place_x(shard_of(partner[k], 1 - core, -d), 1 - s), sibx_recv.at[partner[k]])
         add_chip(k, last=k == 4)
     for copy in sent:
@@ -382,11 +415,6 @@
     shards = 2 * RING
     rows = jnp.stack([conv_bias, ln_gain, ln_bias])
     conv = jnp.concatenate([conv_weight, jnp.pad(rows, ((0, 13), (0, 0)))], axis=0)
-    order = np.arange(tokens).reshape(channels, patches)
-    natural = np.eye(tokens, dtype=ml_dtypes.bfloat16)
-    patch_major = natural[order.T.reshape(-1)]
-    to_role = jnp.where(s == 0, jnp.asarray(patch_major), jnp.asarray(natural))
-    to_own = jnp.where(s == 0, jnp.asarray(patch_major.T), jnp.asarray(natural))
     patch_of = np.arange(2 * channels) // channels
     mask_a = (patch_of[:, None] == patch_of[None]).astype(np.float32)
     channel_of = np.tile(np.arange(8 * patches) // patches, 2)
@@ -397,9 +425,9 @@
     bf16 = jnp.bfloat16
     flops = 4 * tokens * (width * samples + half * 3 * half + width * width // 2)
     mixed = pl.pallas_call(
-        night_kernel,
+        functools.partial(night_kernel, channels, patches),
         out_shape=jax.ShapeDtypeStruct((tokens, width), bf16),
-        in_specs=[vmem, anywhere, anywhere, anywhere, anywhere, vmem, vmem, vmem, vmem],
+        in_specs=[vmem, anywhere, anywhere, anywhere, anywhere, vmem, vmem],
         out_specs=vmem,
         scratch_shapes=[
             pltpu.VMEM((2, tokens, samples), bf16),
@@ -413,16 +441,18 @@
             pltpu.VMEM((tokens, half), bf16),
             pltpu.VMEM((tokens, width), bf16),
             pltpu.VMEM((tokens, width), jnp.float32),
-            dma((3, 8)), dma((3, 8)), dma((3, 8)), dma((3, 8)),
+            pltpu.VMEM((tokens, tokens), bf16),
+            pltpu.VMEM((tokens, tokens), bf16),
+            dma((5, 8)), dma((5, 8)), dma((5, 8)), dma((5, 8)),
             dma((8,)), dma((8,)), dma((8,)), dma((8,)), dma((3,)), dma((2,)), dma((4,)), dma((4,)),
         ],
         compiler_params=pltpu.CompilerParams(
             collective_id=0, has_side_effects=True, vmem_limit_bytes=60 * 2**20
         ),
         cost_estimate=pl.CostEstimate(flops=flops, bytes_accessed=2**23, transcendentals=2**21),
-    )(signal.reshape(tokens, samples), conv, w_space, w_time, w_out, to_role, to_own,
-      jnp.asarray(mask_a), jnp.asarray(mask_b))
-    return mixed.reshape(1, channels, patches, width)
+    )(signal.transpose(0, 2, 1, 3).reshape(tokens, samples), conv, w_space, w_time, w_out, jnp.asarray(mask_a),
+      jnp.asarray(mask_b))
+    return mixed.reshape(1, patches, channels, width).transpose(0, 2, 1, 3)
 
 
 def solution(mesh):

time: 150 us -> 139 us (0.927); the launches traced: 148 us -> 139 us
  local copies, waits for them, and re-layouts: 12.5 us -> 3.56 us
  other arithmetic: 4.63 us -> 2.17 us
  Pallas kernels: 131 us -> 133 us
    reshape x3 -> x0, local copies, waits for them, and re-layouts: 11.4 us -> none  [the longest x2 10.5 us: split_by_branch(): return mixed.reshape(1, channels, patches, width)]
    select_n x1 -> x0, other arithmetic: 2.47 us -> none  [split_by_branch(): to_own = jnp.where(s == 0, jnp.asarray(patch_major.T), jnp.asarray(natural))]
    unnamed x1, local copies, waits for them, and re-layouts: 1.16 us -> 3.56 us
    pallas_call x1, Pallas kernels: 131 us -> 133 us  [split_by_branch(): pl.pallas_call(functools.partial(night_kernel, channels, patches), out_sh...]
where the time goes in v2:
time: 139 us
  Pallas kernels  133 us (96%)
  local copies, waits for them, and re-layouts  3.56 us (3%)
  other arithmetic  2.17 us (2%)
    pallas_call x1, Pallas kernels, split_by_branch(): pl.pallas_call(functools.partial(night_kernel, channels, patches), out_sh...  133 us
    unnamed x1, local copies, waits for them, and re-layouts  3.56 us

profile of v2, /device:TPU:6, one launch (start us, length us, event | category | flops | bytes accessed | tf_op | source)
XLA Modules:
  0.0 138.8 jit_solution(5041248118671882786)
XLA Ops:
  0.0 0.7 fusion.4
  0.7 1.5 %pad_maximum_fusion.conv_ref = bf16[272,128]{1,0:T(8,128)(2,1)} fusion(bf16[16,128]{1,0:T(8,128)(2,1)S(1)} %fusion.4, bf16[256,128]{1,0:T(8,128)(2,1)} %param.11), kind=kLoop, calls=%fused_computation | loop fusion | flops 139264 | bytes 139264 | tf_op jit(solution)/shard_map/concatenate | solution.py:417
  2.2 133.1 %shard_map.100 = bf16[640,2048]{1,0:T(8,128)(2,1)} custom-call(bf16[640,256]{1,0:T(8,128)(2,1)} %bitcast.13, bf16[272,128]{1,0:T(8,128)(2,1)} %pad_maximum_fusion.conv_ref, bf16[64,3072]{1,0:T(8,128)(2,1)} %space_ref.1, bf16[64,3072]{1,0:T(8,128)(2,1)} %time_ref.1, bf16[128,2048]{1,0:T(8,128)(2,1)} %out_ref.1, f32[128,128]{1,0:T(8,128)} %constant.7.clone.mask_a_ref, ...), custom_call_target="tpu_custom_call" | custom-call | flops 14763950080 | bytes 8388608 | tf_op jit(solution)/shard_map/pallas_call | solution.py:427
  135.3 3.6 %copy.12 = bf16[1,64,10,2048]{3,1,2,0:T(8,128)(2,1)} copy(bf16[1,64,10,2048]{3,1,2,0:T(8,128)(2,1)} %bitcast.9) | data formatting | bytes 5242880

commit v3 on v2

--- a/solution.py
+++ b/solution.py
@@ -250,7 +250,8 @@
         scores = jnp.where(allowed, scores, -jnp.inf)
         highest = jnp.max(scores, axis=-1, keepdims=True)
         expo = jnp.exp(scores - highest)
-        probs = (expo / jnp.sum(expo, axis=-1, keepdims=True)).astype(jnp.bfloat16)
+        inverse = 1.0 / jnp.sum(expo, axis=-1, keepdims=True)
+        probs = (expo * inverse).astype(jnp.bfloat16)
         return jnp.dot(probs, v, preferred_element_type=jnp.float32).astype(jnp.bfloat16)
 
     def heads(j, between=lambda: None):
@@ -269,7 +270,7 @@
         def _():
             count = mask_a_ref.shape[0]
 
-            @pl.loop(0, 2 * tokens // count)
+            @pl.loop(0, 2 * tokens // count, unroll=2)
             def _(g):
                 rows = pl.ds(pl.multiple_of(g * count, count), count)
                 allowed = mask_a_ref[...] > 0
@@ -285,7 +286,7 @@
         def _():
             count = mask_b_ref.shape[0] // 2
 
-            @pl.loop(0, tokens // count)
+            @pl.loop(0, tokens // count, unroll=2)
             def _(g):
                 first = pl.ds(pl.multiple_of(g * count, 16), count)
                 second = pl.ds(pl.multiple_of(tokens + g * count, 16), count)

time: 139 us -> 136 us (0.978)
  Pallas kernels: 133 us -> 131 us
    pallas_call x1, Pallas kernels: 133 us -> 131 us  [split_by_branch(): pl.pallas_call(functools.partial(night_kernel, channels, patches), out_sh...]
where the time goes in v3:
time: 136 us
  Pallas kernels  131 us (96%)
  local copies, waits for them, and re-layouts  3.56 us (3%)
  other arithmetic  2.17 us (2%)
    pallas_call x1, Pallas kernels, split_by_branch(): pl.pallas_call(functools.partial(night_kernel, channels, patches), out_sh...  131 us
    unnamed x1, local copies, waits for them, and re-layouts  3.56 us

profile of v3, /device:TPU:6, one launch (start us, length us, event | category | flops | bytes accessed | tf_op | source)
XLA Modules:
  0.0 136.2 jit_solution(14898882206749699367)
XLA Ops:
  0.0 0.7 fusion.4
  0.7 1.5 %pad_maximum_fusion.conv_ref = bf16[272,128]{1,0:T(8,128)(2,1)} fusion(bf16[16,128]{1,0:T(8,128)(2,1)S(1)} %fusion.4, bf16[256,128]{1,0:T(8,128)(2,1)} %param.11), kind=kLoop, calls=%fused_computation | loop fusion | flops 139264 | bytes 139264 | tf_op jit(solution)/shard_map/concatenate | solution.py:418
  2.2 130.5 %shard_map.100 = bf16[640,2048]{1,0:T(8,128)(2,1)} custom-call(bf16[640,256]{1,0:T(8,128)(2,1)} %bitcast.13, bf16[272,128]{1,0:T(8,128)(2,1)} %pad_maximum_fusion.conv_ref, bf16[64,3072]{1,0:T(8,128)(2,1)} %space_ref.1, bf16[64,3072]{1,0:T(8,128)(2,1)} %time_ref.1, bf16[128,2048]{1,0:T(8,128)(2,1)} %out_ref.1, f32[128,128]{1,0:T(8,128)} %constant.7.clone.mask_a_ref, ...), custom_call_target="tpu_custom_call" | custom-call | flops 14763950080 | bytes 8388608 | tf_op jit(solution)/shard_map/pallas_call | solution.py:428
  132.7 3.6 %copy.12 = bf16[1,64,10,2048]{3,1,2,0:T(8,128)(2,1)} copy(bf16[1,64,10,2048]{3,1,2,0:T(8,128)(2,1)} %bitcast.9) | data formatting | bytes 5242880
